TPU v7x, 32 devices: a whole 2x2x4 slice. The times are simulated.
32 devices in a mesh: mp: 4 (over z), ffn: 8 (over y, x, core).
Axes of the slice: x: 2, y: 2, z: 4, core: 2. Of those that a mesh axis runs over, the one named last changes fastest.
Arguments:
- tokens: bfloat16 [1024, 8192], P('ffn', 'mp'), may hold values from -6 to 6
- gate_weight: bfloat16 [8192, 28672], P('mp', 'ffn'), may hold values from -0.0625 to 0.0625
- up_weight: bfloat16 [8192, 28672], P('mp', 'ffn'), may hold values from -0.0625 to 0.0625
- down_weight: bfloat16 [28672, 8192], P('ffn', 'mp'), may hold values from -0.03125 to 0.03125
Outputs:
- mixed: bfloat16 [1024, 8192], P('ffn', 'mp')
All inputs are finite; a program needn't handle non-finite values.
Results may differ from a plain program's by a relative error of at most 0.03.
Values may be sent and summed in bfloat16 or wider, within the bound.
A program may use at most 128 MiB of HBM per device.

v0:
```python
import functools

import jax
import jax.numpy as jnp
from jax import lax
from jax.experimental import pallas as pl
from jax.experimental.pallas import tpu as pltpu
from jax.sharding import PartitionSpec as P

ROWS = 32
GROUP = 2
SLOTS = 8
MESH = pl.DeviceIdType.MESH


def widest(columns, most=1024):
    return max(w for w in range(128, most + 1, 128) if columns % w == 0)


def xor(a, b, size):
    total, bit = 0, 1
    while bit < size:
        total = total + lax.rem(lax.div(a, bit) + lax.div(b, bit), 2) * bit
        bit *= 2
    return total


def kernel(n, peers, tokens, w_gate, w_up, w_down, out, landed, tok, gate_w, up_w, down_w,
           sum_a, sum_b, part_a, part_b, hid_a, hid_b, mine, outgoing,
           load_sem, tok_send, tok_recv, sum_send, sum_recv, credit, hid_send, hid_recv, out_send, out_recv):
    f32, bf16 = jnp.float32, jnp.bfloat16
    m, f = lax.axis_index("mp"), lax.axis_index("ffn")
    pieces = tokens.shape[0]
    blocks = pieces * peers
    chunks = blocks * GROUP
    half = sum_a.shape[2] // 2
    width = mine.shape[2]
    last = n - 1
    sums, parts, hids = (sum_a, sum_b), (part_a, part_b), (hid_a, hid_b)
    depths = (m, last - m)
    ahead = (m + 1, m - 1)
    behind = (m - 1, m + 1)

    def turn(p):
        return 1 if p == peers - 1 else p + 1

    def half_loads(d):
        columns = pl.ds(d * half, half)
        return (pltpu.make_async_copy(w_gate.at[:, columns], gate_w.at[:, columns], load_sem.at[2 * d]),
                pltpu.make_async_copy(w_up.at[:, columns], up_w.at[:, columns], load_sem.at[2 * d + 1]))

    down_load = pltpu.make_async_copy(w_down, down_w, load_sem.at[4])
    own_load = pltpu.make_async_copy(tokens, tok.at[pl.ds(0, pieces)], load_sem.at[5])
    own_load.start()

    @pl.when(depths[0] <= depths[1])
    def _():
        for load in half_loads(0) + half_loads(1):
            load.start()

    @pl.when(depths[0] > depths[1])
    def _():
        for load in half_loads(1) + half_loads(0):
            load.start()

    barrier = pltpu.get_barrier_semaphore()
    for p in range(1, peers):
        pl.semaphore_signal(barrier, inc=1, device_id={"ffn": xor(f, turn(p), peers)}, device_id_type=MESH)

    @pl.when(m > 0)
    def _():
        pl.semaphore_signal(barrier, inc=1, device_id={"mp": m - 1}, device_id_type=MESH)

    @pl.when(m < last)
    def _():
        pl.semaphore_signal(barrier, inc=1, device_id={"mp": m + 1}, device_id_type=MESH)

    pl.semaphore_wait(barrier, peers - 1 + jnp.where(m > 0, 1, 0) + jnp.where(m < last, 1, 0))

    def block_of(c):
        return lax.div(c, GROUP)

    def rows_of(c):
        return pl.ds(pl.multiple_of(lax.rem(c, GROUP) * ROWS, ROWS), ROWS)

    def token_copy(p, peer):
        return pltpu.make_async_remote_copy(
            src_ref=tokens, dst_ref=tok.at[pl.ds(p * pieces, pieces)],
            send_sem=tok_send.at[p], recv_sem=tok_recv.at[p],
            device_id={"ffn": peer}, device_id_type=MESH)

    def sum_copy(d, c):
        slot = lax.rem(c, SLOTS)
        return pltpu.make_async_remote_copy(
            src_ref=sums[d].at[slot], dst_ref=sums[d].at[slot],
            send_sem=sum_send.at[d, lax.rem(c, 2)], recv_sem=sum_recv.at[d, slot],
            device_id={"mp": ahead[d]}, device_id_type=MESH)

    def hid_copy(d, c):
        return pltpu.make_async_remote_copy(
            src_ref=hids[d].at[block_of(c), rows_of(c)], dst_ref=hids[d].at[block_of(c), rows_of(c)],
            send_sem=hid_send.at[d, lax.rem(c, 2)], recv_sem=hid_recv.at[d, c],
            device_id={"mp": behind[d]}, device_id_type=MESH)

    def out_copy(b, peer):
        return pltpu.make_async_remote_copy(
            src_ref=outgoing.at[lax.rem(b, 2)], dst_ref=landed.at[b],
            send_sem=out_send.at[lax.rem(b, 2)], recv_sem=out_recv.at[b],
            device_id={"ffn": peer}, device_id_type=MESH)

    for p in range(1, peers):
        token_copy(p, xor(f, turn(p), peers)).start()
    down_load.start()

    def first_matmul(d, c):
        tile = widest(half)

        @pl.when(c == 0)
        def _():
            for load in half_loads(d):
                load.wait()

        @pl.when((c >= 0) & (c < chunks) & (lax.rem(jnp.maximum(c, 0), GROUP) == 0))
        def _():
            @pl.loop(0, half // tile)
            def _(j):
                x = tok[block_of(c)]
                to = pl.multiple_of(j * tile, tile)
                columns = pl.ds(pl.multiple_of(d * half + j * tile, 128), tile)
                parts[d][:, pl.ds(to, tile)] = jnp.dot(
                    x, gate_w[:, columns], preferred_element_type=f32).astype(bf16)
                parts[d][:, pl.ds(pl.multiple_of(half + j * tile, 128), tile)] = jnp.dot(
                    x, up_w[:, columns], preferred_element_type=f32).astype(bf16)

    def first_matmuls(s):
        q = s - jnp.minimum(depths[0], depths[1])

        held = pieces * GROUP

        @pl.when((q >= held) & (q < chunks) & (lax.rem(jnp.maximum(q, 0), held) == 0))
        def _():
            token_copy(lax.div(q, held), f).wait_recv()

        for d in range(2):
            first_matmul(d, s - depths[d])

    def pass_sum(d, s):
        c = s - depths[d]
        depth, slots, part = depths[d], sums[d], parts[d]

        @pl.when((c >= 0) & (c < chunks))
        def _():
            slot, own = lax.rem(c, SLOTS), rows_of(c)

            @pl.when(depth == 0)
            def _():
                slots[slot] = part[own, :]

            @pl.when(depth > 0)
            def _():
                sum_copy(d, c).wait_recv()

            @pl.when((depth > 0) & (depth < last))
            def _():
                slots[slot] = (slots[slot].astype(f32) + part[own, :].astype(f32)).astype(bf16)

            @pl.when(depth < last)
            def _():
                @pl.when(c >= SLOTS)
                def _():
                    pl.semaphore_wait(credit.at[d], 1)

                sum_copy(d, c).start()

            @pl.when(depth == last)
            def _():
                gate = slots[slot, :, :half].astype(f32) + part[own, :half].astype(f32)
                up = slots[slot, :, half:].astype(f32) + part[own, half:].astype(f32)
                hids[d][block_of(c), own, :] = (gate / (1.0 + jnp.exp(-gate)) * up).astype(bf16)
                hid_copy(d, c).start()

                @pl.when(c + SLOTS < chunks)
                def _():
                    pl.semaphore_signal(credit.at[d], inc=1, device_id={"mp": behind[d]}, device_id_type=MESH)

    def pass_hidden(d, s):
        depth = depths[d]
        c = s - (2 * last - depth)

        @pl.when((depth < last) & (c >= 0) & (c < chunks))
        def _():
            hid_copy(d, c).wait_recv()

            @pl.when(depth > 0)
            def _():
                hid_copy(d, c).start()

    def sent(d, s):
        depth = depths[d]
        c = s - depth - 1

        @pl.when((depth < last) & (c >= 0) & (c < chunks))
        def _():
            sum_copy(d, c).wait_send()

            @pl.when((depth > 0) & (c + SLOTS < chunks))
            def _():
                pl.semaphore_signal(credit.at[d], inc=1, device_id={"mp": behind[d]}, device_id_type=MESH)

        h = s - (2 * last - depth) - 1

        @pl.when((depth > 0) & (h >= 0) & (h < chunks))
        def _():
            hid_copy(d, h).wait_send()

    def second_matmul(s):
        c = s - jnp.maximum(2 * last - m, last + m) - (GROUP - 1)
        b = block_of(jnp.maximum(c, 0))
        part = lax.rem(jnp.maximum(c, 0), GROUP)
        share = width // GROUP
        tile = widest(share)
        ready = (c >= 0) & (c < chunks)

        def product(j):
            columns = pl.ds(pl.multiple_of(part * share + j * tile, tile), tile)
            total = jnp.dot(hid_a[b], down_w[pl.ds(0, half), columns], preferred_element_type=f32)
            total += jnp.dot(hid_b[b], down_w[pl.ds(half, half), columns], preferred_element_type=f32)
            return columns, total.astype(bf16)

        @pl.when(c == 0)
        def _():
            down_load.wait()

        @pl.when(ready & (b < pieces))
        def _():
            @pl.loop(0, share // tile)
            def _(j):
                columns, total = product(j)
                mine[b, :, columns] = total

        @pl.when(ready & (b >= pieces))
        def _():
            p = lax.div(b, pieces)
            peer = xor(f, jnp.where(p == peers - 1, 1, p + 1), peers)
            par = lax.rem(b, 2)

            @pl.when((b >= pieces + 2) & (part == 0))
            def _():
                out_copy(b, peer).wait_send()

            @pl.loop(0, share // tile)
            def _(j):
                columns, total = product(j)
                outgoing[par, :, columns] = total

            @pl.when(part == GROUP - 1)
            def _():
                out_copy(b, peer).start()

    own_load.wait()
    first_matmuls(jnp.int32(0))

    @pl.loop(0, chunks + 2 * last + GROUP - 1)
    def _(s):
        pass_sum(0, s)
        pass_sum(1, s)
        sent(0, s)
        sent(1, s)
        first_matmuls(s + 1)
        pass_hidden(0, s)
        pass_hidden(1, s)
        second_matmul(s)

    for p in range(1, peers):
        token_copy(p, f).wait_send()
    for b in range(pieces, blocks):
        out_copy(b, f).wait_recv()
        pltpu.make_async_copy(landed.at[b], tok.at[b], out_recv.at[b]).start()
    for b in range(pieces, blocks):
        pltpu.make_async_copy(landed.at[b], tok.at[b], out_recv.at[b]).wait()
    for k in range(pieces):
        total = mine[k].astype(f32)
        for p in range(1, peers):
            total += tok[p * pieces + k].astype(f32)
        out[k] = total.astype(bf16)
    for b in range(blocks - min(2, blocks - pieces), blocks):
        out_copy(b, f).wait_send()


def on_device(n, peers, tokens, gate_weight, up_weight, down_weight):
    held, depth = tokens.shape
    hidden, width = down_weight.shape
    rows, half = ROWS * GROUP, hidden // 2
    pieces = held // rows
    blocks = pieces * peers
    chunks = blocks * GROUP
    bf16 = jnp.bfloat16
    dma = pltpu.SemaphoreType.DMA
    flops = 6 * blocks * rows * depth * hidden
    out, _ = pl.pallas_call(
        functools.partial(kernel, n, peers),
        out_shape=(jax.ShapeDtypeStruct((pieces, rows, width), bf16),
                   jax.ShapeDtypeStruct((blocks, rows, width), bf16)),
        in_specs=[pl.BlockSpec(memory_space=pl.ANY)] * 4,
        out_specs=(pl.BlockSpec(memory_space=pltpu.VMEM), pl.BlockSpec(memory_space=pl.ANY)),
        scratch_shapes=[
            pltpu.VMEM((blocks, rows, depth), bf16),
            pltpu.VMEM((depth, hidden), bf16),
            pltpu.VMEM((depth, hidden), bf16),
            pltpu.VMEM((hidden, width), bf16),
            pltpu.VMEM((SLOTS, ROWS, hidden), bf16),
            pltpu.VMEM((SLOTS, ROWS, hidden), bf16),
            pltpu.VMEM((rows, hidden), bf16),
            pltpu.VMEM((rows, hidden), bf16),
            pltpu.VMEM((blocks, rows, half), bf16),
            pltpu.VMEM((blocks, rows, half), bf16),
            pltpu.VMEM((pieces, rows, width), bf16),
            pltpu.VMEM((2, rows, width), bf16),
            dma((6,)), dma((peers,)), dma((peers,)), dma((2, 2)), dma((2, SLOTS)),
            pltpu.SemaphoreType.REGULAR((2,)), dma((2, 2)), dma((2, chunks)), dma((2,)), dma((blocks,)),
        ],
        compiler_params=pltpu.CompilerParams(
            collective_id=0, has_side_effects=True, vmem_limit_bytes=63 * 1024 * 1024),
        cost_estimate=pl.CostEstimate(
            flops=flops, bytes_accessed=6 * depth * hidden, transcendentals=blocks * rows * half),
    )(tokens.reshape(pieces, rows, depth), gate_weight, up_weight, down_weight)
    return out.reshape(held, width)


def solution(mesh):
    in_specs = (P("ffn", "mp"), P("mp", "ffn"), P("mp", "ffn"), P("ffn", "mp"))
    body = functools.partial(on_device, mesh.shape["mp"], mesh.shape["ffn"])
    return jax.shard_map(body, mesh=mesh, in_specs=in_specs, out_specs=P("ffn", "mp"), check_vma=False)
```

profile of v0, /device:TPU:0, one launch (start us, length us, event | category | flops | bytes accessed | tf_op | source)
XLA Modules:
  0.0 277.1 jit_solution(1021550395744945580)
XLA Ops:
  0.0 275.3 %shard_map.46 = (bf16[2,64,2048]{2,1,0:T(8,128)(2,1)}, bf16[16,64,2048]{2,1,0:T(8,128)(2,1)}) custom-call(bf16[2,64,2048]{2,1,0:T(8,128)(2,1)} %bitcast.3, bf16[2048,3584]{1,0:T(8,128)(2,1)} %w_gate.1, bf16[2048,3584]{1,0:T(8,128)(2,1)} %w_up.1, bf16[3584,2048]{1,0:T(8,128)(2,1)} %w_down.1), custom_call_target="tpu_custom_call" | custom-call | flops 45097156608 | bytes 44040192 | tf_op jit(solution)/shard_map/pallas_call | solution.py:300
  275.3 1.9 copy.6
where the time goes:
time: 277 us
  Pallas kernels  275 us (99%)
    pallas_call x1, Pallas kernels, on_device(): pl.pallas_call(functools.partial(kernel, n, peers), out_shape=(jax.ShapeD...  275 us

commit v1 on v0

v1 whole, which is shorter than its diff:
```python
import functools

import jax
import jax.numpy as jnp
from jax import lax
from jax.experimental import pallas as pl
from jax.experimental.pallas import tpu as pltpu
from jax.sharding import PartitionSpec as P

SLOTS = 12
STRIDE = 2
LAG = 0
SENDS = 3
PREFETCH = 3
MESH = pl.DeviceIdType.MESH


def widest(columns, most):
    return max(w for w in range(128, most + 1, 128) if columns % w == 0)


def xor(a, b, size):
    total, bit = 0, 1
    while bit < size:
        total = total + lax.rem(lax.div(a, bit) + lax.div(b, bit), 2) * bit
        bit *= 2
    return total


def kernel(n, peers, tokens, w_gate, w_up, w_down, out, tok, first_w, down_w,
           sum_a, sum_b, part_a, part_b, hid_a, hid_b, acc, mine, outgoing,
           load_sem, own_sem, tok_send, tok_recv, sum_send, sum_recv, credit, hid_send, hid_recv,
           out_send, out_recv, free):
    f32, bf16 = jnp.float32, jnp.bfloat16
    m, f = lax.axis_index("mp"), lax.axis_index("ffn")
    chunks, _, cols = hid_a.shape
    groups = chunks // peers
    half = groups * cols
    width = acc.shape[1]
    tile = widest(width, 512)
    tiles = width // tile
    last = n - 1
    sums, parts, hids = (sum_a, sum_b), (part_a, part_b), (hid_a, hid_b)
    depths = (m, last - m)
    ahead = (m + 1, m - 1)
    behind = (m - 1, m + 1)

    def peer_of(p):
        return xor(f, jnp.where(p == peers - 1, 1, p + 1), peers)

    def group_loads(d, j):
        columns = pl.ds(pl.multiple_of(d * half + j * cols, 128), cols)
        return (pltpu.make_async_copy(w_gate.at[:, columns], first_w.at[d * groups + j, :, pl.ds(0, cols)],
                                      load_sem.at[d, 0, j]),
                pltpu.make_async_copy(w_up.at[:, columns], first_w.at[d * groups + j, :, pl.ds(cols, cols)],
                                      load_sem.at[d, 1, j]))

    own_load = pltpu.make_async_copy(tokens, tok.at[0], own_sem.at[0])
    down_load = pltpu.make_async_copy(w_down, down_w, own_sem.at[1])
    own_load.start()

    @pl.when(depths[0] <= depths[1])
    def _():
        for load in group_loads(0, 0) + group_loads(1, 0):
            load.start()

    @pl.when(depths[0] > depths[1])
    def _():
        for load in group_loads(1, 0) + group_loads(0, 0):
            load.start()

    for j in range(1, min(PREFETCH, groups)):
        for load in group_loads(0, j) + group_loads(1, j):
            load.start()

    barrier = pltpu.get_barrier_semaphore()
    for p in range(1, peers):
        pl.semaphore_signal(barrier, inc=1, device_id={"ffn": peer_of(p)}, device_id_type=MESH)

    @pl.when(m > 0)
    def _():
        pl.semaphore_signal(barrier, inc=1, device_id={"mp": m - 1}, device_id_type=MESH)

    @pl.when(m < last)
    def _():
        pl.semaphore_signal(barrier, inc=1, device_id={"mp": m + 1}, device_id_type=MESH)

    pl.semaphore_wait(barrier, peers - 1 + jnp.where(m > 0, 1, 0) + jnp.where(m < last, 1, 0))

    def token_copy(p, peer):
        return pltpu.make_async_remote_copy(
            src_ref=tokens, dst_ref=tok.at[p],
            send_sem=tok_send.at[p], recv_sem=tok_recv.at[p],
            device_id={"ffn": peer}, device_id_type=MESH)

    def sum_copy(d, c):
        slot = lax.rem(c, SLOTS)
        return pltpu.make_async_remote_copy(
            src_ref=sums[d].at[slot], dst_ref=sums[d].at[slot],
            send_sem=sum_send.at[d, lax.rem(c, SENDS)], recv_sem=sum_recv.at[d, slot],
            device_id={"mp": ahead[d]}, device_id_type=MESH)

    def hid_copy(d, c):
        return pltpu.make_async_remote_copy(
            src_ref=hids[d].at[c], dst_ref=hids[d].at[c],
            send_sem=hid_send.at[d, lax.rem(c, SENDS)], recv_sem=hid_recv.at[d, c],
            device_id={"mp": behind[d]}, device_id_type=MESH)

    def out_copy(p, t, peer):
        columns = pl.ds(pl.multiple_of(t * tile, 128), tile)
        return pltpu.make_async_remote_copy(
            src_ref=outgoing.at[lax.rem(p, 2), :, columns], dst_ref=tok.at[p, :, columns],
            send_sem=out_send.at[lax.rem(p, 2), t], recv_sem=out_recv.at[p, t],
            device_id={"ffn": peer}, device_id_type=MESH)

    token_copy(1, peer_of(1)).start()

    def start_loads(s):
        g = s + PREFETCH

        @pl.when(g < groups)
        def _():
            for load in group_loads(0, g) + group_loads(1, g):
                load.start()

        @pl.when(g == groups)
        def _():
            down_load.start()

        q = s - groups // 2
        p = lax.div(q, groups) + 2

        @pl.when((q >= 0) & (lax.rem(q, groups) == 0) & (p < peers))
        def _():
            token_copy(p, peer_of(p)).start()

    def first_matmul(d, c):
        @pl.when((c >= 0) & (c < groups))
        def _():
            for load in group_loads(d, c):
                load.wait()

        @pl.when((c >= 0) & (c < chunks))
        def _():
            parts[d][...] = jnp.dot(
                tok[lax.div(c, groups)], first_w[d * groups + lax.rem(c, groups)],
                preferred_element_type=f32).astype(bf16)

    def first_matmuls(s):
        q = s - STRIDE * jnp.minimum(depths[0], depths[1])

        @pl.when((q >= groups) & (q < chunks) & (lax.rem(q, groups) == 0))
        def _():
            token_copy(lax.div(q, groups), f).wait_recv()

        for d in range(2):
            first_matmul(d, s - STRIDE * depths[d])

        e = s - STRIDE * jnp.maximum(depths[0], depths[1]) + 1
        p = lax.div(e, groups) - 1

        @pl.when((p >= 1) & (e <= chunks) & (lax.rem(e, groups) == 0))
        def _():
            pl.semaphore_signal(free.at[p], inc=1, device_id={"ffn": peer_of(p)}, device_id_type=MESH)

    def pass_sum(d, s):
        depth, slots, part = depths[d], sums[d], parts[d]
        c = s - STRIDE * depth

        @pl.when((c >= 0) & (c < chunks))
        def _():
            slot = lax.rem(c, SLOTS)

            @pl.when(depth > 0)
            def _():
                sum_copy(d, c).wait_recv()

            @pl.when(depth < last)
            def _():
                @pl.when(c >= SLOTS)
                def _():
                    pl.semaphore_wait(credit.at[d], 1)

                @pl.when(depth == 0)
                def _():
                    slots[slot] = part[...]

                @pl.when(depth > 0)
                def _():
                    slots[slot] = (slots[slot].astype(f32) + part[...].astype(f32)).astype(bf16)

                sum_copy(d, c).start()

            @pl.when(depth == last)
            def _():
                gate = slots[slot, :, :cols].astype(f32) + part[:, :cols].astype(f32)
                up = slots[slot, :, cols:].astype(f32) + part[:, cols:].astype(f32)
                hids[d][c] = (gate / (1.0 + jnp.exp(-gate)) * up).astype(bf16)

                @pl.when(c + SLOTS < chunks)
                def _():
                    pl.semaphore_signal(credit.at[d], inc=1, device_id={"mp": behind[d]}, device_id_type=MESH)

    def pass_hidden(d, s):
        depth = depths[d]
        c = s - STRIDE * (2 * last - depth) - LAG

        @pl.when((c >= 0) & (c < chunks))
        def _():
            @pl.when(depth < last)
            def _():
                hid_copy(d, c).wait_recv()

            @pl.when(depth > 0)
            def _():
                hid_copy(d, c).start()

    def sent(d, s):
        depth = depths[d]
        c = s - STRIDE * depth - (SENDS - 1)

        @pl.when((depth < last) & (c >= 0) & (c < chunks))
        def _():
            sum_copy(d, c).wait_send()

            @pl.when((depth > 0) & (c + SLOTS < chunks))
            def _():
                pl.semaphore_signal(credit.at[d], inc=1, device_id={"mp": behind[d]}, device_id_type=MESH)

        h = s - STRIDE * (2 * last - depth) - LAG - (SENDS - 1)

        @pl.when((depth > 0) & (h >= 0) & (h < chunks))
        def _():
            hid_copy(d, h).wait_send()

    def second_matmul(s):
        c = s - STRIDE * jnp.maximum(2 * last - m, last + m) - LAG

        @pl.when(c == 0)
        def _():
            down_load.wait()

        @pl.when((c >= 0) & (c < chunks))
        def _():
            b, j = lax.div(c, groups), lax.rem(c, groups)
            peer = peer_of(b)

            @pl.when((j == groups - 1) & (b > 0))
            def _():
                pl.semaphore_wait(free.at[b], 1)

            @pl.when(j == 0)
            def _():
                acc[...] = jnp.zeros_like(acc)

            @pl.loop(0, tiles)
            def _(t):
                columns = pl.ds(pl.multiple_of(t * tile, 128), tile)
                total = jnp.dot(hid_a[c], down_w[j, :, columns], preferred_element_type=f32)
                total += jnp.dot(hid_b[c], down_w[groups + j, :, columns], preferred_element_type=f32)
                acc[:, columns] += total

                @pl.when((j == groups - 1) & (b == 0))
                def _():
                    mine[:, columns] = acc[:, columns]

                @pl.when((j == groups - 1) & (b > 0))
                def _():
                    @pl.when(b > 2)
                    def _():
                        out_copy(b - 2, t, peer).wait_send()

                    outgoing[lax.rem(b, 2), :, columns] = acc[:, columns].astype(bf16)
                    out_copy(b, t, peer).start()

            @pl.when((j == min(2, groups - 1)) & (b > 1))
            def _():
                @pl.loop(0, tiles)
                def _(t):
                    columns = pl.ds(pl.multiple_of(t * tile, 128), tile)
                    out_copy(b - 1, t, f).wait_recv()
                    mine[:, columns] += tok[b - 1, :, columns].astype(f32)

    own_load.wait()
    first_matmuls(jnp.int32(0))

    @pl.loop(0, chunks + 2 * STRIDE * last + LAG + max(0, SENDS - 1 - STRIDE))
    def _(s):
        start_loads(s)
        pass_sum(0, s)
        pass_sum(1, s)
        sent(0, s)
        sent(1, s)
        pass_hidden(0, s)
        pass_hidden(1, s)
        first_matmuls(s + 1)
        second_matmul(s)

    for t in range(tiles):
        columns = pl.ds(t * tile, tile)
        out_copy(peers - 1, t, f).wait_recv()
        out[:, columns] = (mine[:, columns] + tok[peers - 1, :, columns].astype(f32)).astype(bf16)
    for p in range(1, peers):
        token_copy(p, f).wait_send()
    for p in range(max(1, peers - 2), peers):
        for t in range(tiles):
            out_copy(p, t, f).wait_send()


def on_device(n, peers, tokens, gate_weight, up_weight, down_weight):
    held, depth = tokens.shape
    hidden, width = down_weight.shape
    half = hidden // 2
    cols = widest(half, 256)
    groups = half // cols
    chunks = groups * peers
    bf16, f32 = jnp.bfloat16, jnp.float32
    tiles = width // widest(width, 512)
    dma, regular = pltpu.SemaphoreType.DMA, pltpu.SemaphoreType.REGULAR
    return pl.pallas_call(
        functools.partial(kernel, n, peers),
        out_shape=jax.ShapeDtypeStruct((held, width), bf16),
        in_specs=[pl.BlockSpec(memory_space=pl.ANY)] * 4,
        out_specs=pl.BlockSpec(memory_space=pltpu.VMEM),
        scratch_shapes=[
            pltpu.VMEM((peers, held, depth), bf16),
            pltpu.VMEM((2 * groups, depth, 2 * cols), bf16),
            pltpu.VMEM((2 * groups, cols, width), bf16),
            pltpu.VMEM((SLOTS, held, 2 * cols), bf16),
            pltpu.VMEM((SLOTS, held, 2 * cols), bf16),
            pltpu.VMEM((held, 2 * cols), bf16),
            pltpu.VMEM((held, 2 * cols), bf16),
            pltpu.VMEM((chunks, held, cols), bf16),
            pltpu.VMEM((chunks, held, cols), bf16),
            pltpu.VMEM((held, width), f32),
            pltpu.VMEM((held, width), f32),
            pltpu.VMEM((2, held, width), bf16),
            dma((2, 2, groups)), dma((2,)), dma((peers,)), dma((peers,)), dma((2, SENDS)), dma((2, SLOTS)),
            regular((2,)), dma((2, SENDS)), dma((2, chunks)), dma((2, tiles)), dma((peers, tiles)), regular((peers,)),
        ],
        compiler_params=pltpu.CompilerParams(
            collective_id=0, has_side_effects=True, vmem_limit_bytes=63 * 1024 * 1024),
        cost_estimate=pl.CostEstimate(
            flops=6 * peers * held * depth * hidden, bytes_accessed=6 * depth * hidden,
            transcendentals=peers * held * half),
    )(tokens, gate_weight, up_weight, down_weight.reshape(2 * groups, cols, width))


def solution(mesh):
    in_specs = (P("ffn", "mp"), P("mp", "ffn"), P("mp", "ffn"), P("ffn", "mp"))
    body = functools.partial(on_device, mesh.shape["mp"], mesh.shape["ffn"])
    return jax.shard_map(body, mesh=mesh, in_specs=in_specs, out_specs=P("ffn", "mp"), check_vma=False)
```

time: 277 us -> 270 us (0.975)
  Pallas kernels: 275 us -> 268 us
    pallas_call x1, Pallas kernels: 275 us -> 268 us  [on_device(): pl.pallas_call(functools.partial(kernel, n, peers), out_shape=jax.ShapeDt...]
where the time goes in v1:
time: 270 us; the launch traced here: 269 us
  Pallas kernels  268 us (99%)
    pallas_call x1, Pallas kernels, on_device(): pl.pallas_call(functools.partial(kernel, n, peers), out_shape=jax.ShapeDt...  268 us

profile of v1, /device:TPU:0, one launch (start us, length us, event | category | flops | bytes accessed | tf_op | source)
XLA Modules:
  0.0 269.4 jit_solution(13665502065155011475)
XLA Ops:
  0.0 267.5 %shard_map.46 = bf16[128,2048]{1,0:T(8,128)(2,1)} custom-call(bf16[128,2048]{1,0:T(8,128)(2,1)} %tokens.1, bf16[2048,3584]{1,0:T(8,128)(2,1)} %w_gate.1, bf16[2048,3584]{1,0:T(8,128)(2,1)} %w_up.1, bf16[14,256,2048]{2,1,0:T(8,128)(2,1)} %bitcast.1), custom_call_target="tpu_custom_call" | custom-call | flops 45097156608 | bytes 44040192 | tf_op jit(solution)/shard_map/pallas_call | solution.py:320
  267.5 1.9 copy.6

commit v2 on v1

--- a/solution.py
+++ b/solution.py
@@ -11,7 +11,9 @@
 STRIDE = 2
 LAG = 0
 SENDS = 3
-PREFETCH = 3
+PREFETCH = 2
+TAIL = 2
+COLS = 256
 MESH = pl.DeviceIdType.MESH
 
 
@@ -28,8 +30,8 @@
 
 
 def kernel(n, peers, tokens, w_gate, w_up, w_down, out, tok, first_w, down_w,
-           sum_a, sum_b, part_a, part_b, hid_a, hid_b, acc, mine, outgoing,
-           load_sem, own_sem, tok_send, tok_recv, sum_send, sum_recv, credit, hid_send, hid_recv,
+           sum_a, sum_b, part_a, part_b, hid_a, hid_b, acc, mine, outgoing, result,
+           load_sem, own_sem, result_sem, tok_send, tok_recv, sum_send, sum_recv, credit, hid_send, hid_recv,
            out_send, out_recv, free):
     f32, bf16 = jnp.float32, jnp.bfloat16
     m, f = lax.axis_index("mp"), lax.axis_index("ffn")
@@ -40,6 +42,8 @@
     tile = widest(width, 512)
     tiles = width // tile
     last = n - 1
+    head = groups - min(TAIL, groups - 1)
+    others = (peers - 1) * groups
     sums, parts, hids = (sum_a, sum_b), (part_a, part_b), (hid_a, hid_b)
     depths = (m, last - m)
     ahead = (m + 1, m - 1)
@@ -47,6 +51,12 @@
 
     def peer_of(p):
         return xor(f, jnp.where(p == peers - 1, 1, p + 1), peers)
+
+    def place(c):
+        q = c - head
+        own = (q < 0) | (q >= others)
+        block = jnp.where(own, 0, lax.div(q, groups) + 1)
+        return block, jnp.where(q < 0, c, jnp.where(own, q - others + head, lax.rem(q, groups)))
 
     def group_loads(d, j):
         columns = pl.ds(pl.multiple_of(d * half + j * cols, 128), cols)
@@ -61,16 +71,12 @@
 
     @pl.when(depths[0] <= depths[1])
     def _():
-        for load in group_loads(0, 0) + group_loads(1, 0):
+        for load in group_loads(0, 0):
             load.start()
 
     @pl.when(depths[0] > depths[1])
     def _():
-        for load in group_loads(1, 0) + group_loads(0, 0):
-            load.start()
-
-    for j in range(1, min(PREFETCH, groups)):
-        for load in group_loads(0, j) + group_loads(1, j):
+        for load in group_loads(1, 0):
             load.start()
 
     barrier = pltpu.get_barrier_semaphore()
@@ -113,7 +119,25 @@
             send_sem=out_send.at[lax.rem(p, 2), t], recv_sem=out_recv.at[p, t],
             device_id={"ffn": peer}, device_id_type=MESH)
 
+    def result_copy(t):
+        columns = pl.ds(pl.multiple_of(t * tile, 128), tile)
+        return pltpu.make_async_copy(result.at[:, columns], out.at[:, columns], result_sem.at[t])
+
     token_copy(1, peer_of(1)).start()
+
+    @pl.when(depths[0] <= depths[1])
+    def _():
+        for load in group_loads(1, 0):
+            load.start()
+
+    @pl.when(depths[0] > depths[1])
+    def _():
+        for load in group_loads(0, 0):
+            load.start()
+
+    for j in range(1, min(PREFETCH, groups)):
+        for load in group_loads(0, j) + group_loads(1, j):
+            load.start()
 
     def start_loads(s):
         g = s + PREFETCH
@@ -135,31 +159,31 @@
             token_copy(p, peer_of(p)).start()
 
     def first_matmul(d, c):
-        @pl.when((c >= 0) & (c < groups))
-        def _():
-            for load in group_loads(d, c):
+        b, j = place(c)
+
+        @pl.when(((c >= 0) & (c < head)) | ((b == 1) & (j >= head)))
+        def _():
+            for load in group_loads(d, j):
                 load.wait()
 
         @pl.when((c >= 0) & (c < chunks))
         def _():
             parts[d][...] = jnp.dot(
-                tok[lax.div(c, groups)], first_w[d * groups + lax.rem(c, groups)],
-                preferred_element_type=f32).astype(bf16)
+                tok[b], first_w[d * groups + j], preferred_element_type=f32).astype(bf16)
 
     def first_matmuls(s):
-        q = s - STRIDE * jnp.minimum(depths[0], depths[1])
-
-        @pl.when((q >= groups) & (q < chunks) & (lax.rem(q, groups) == 0))
-        def _():
-            token_copy(lax.div(q, groups), f).wait_recv()
+        b, j = place(s - STRIDE * jnp.minimum(depths[0], depths[1]))
+
+        @pl.when((b > 0) & (j == 0))
+        def _():
+            token_copy(b, f).wait_recv()
 
         for d in range(2):
             first_matmul(d, s - STRIDE * depths[d])
 
-        e = s - STRIDE * jnp.maximum(depths[0], depths[1]) + 1
-        p = lax.div(e, groups) - 1
-
-        @pl.when((p >= 1) & (e <= chunks) & (lax.rem(e, groups) == 0))
+        p, k = place(s - STRIDE * jnp.maximum(depths[0], depths[1]))
+
+        @pl.when((p > 0) & (k == groups - 1))
         def _():
             pl.semaphore_signal(free.at[p], inc=1, device_id={"ffn": peer_of(p)}, device_id_type=MESH)
 
@@ -242,27 +266,40 @@
 
         @pl.when((c >= 0) & (c < chunks))
         def _():
-            b, j = lax.div(c, groups), lax.rem(c, groups)
+            b, j = place(c)
             peer = peer_of(b)
 
             @pl.when((j == groups - 1) & (b > 0))
             def _():
                 pl.semaphore_wait(free.at[b], 1)
 
-            @pl.when(j == 0)
+            @pl.when((j == 0) & (b > 0))
             def _():
                 acc[...] = jnp.zeros_like(acc)
+
+            @pl.when(c == 0)
+            def _():
+                mine[...] = jnp.zeros_like(mine)
 
             @pl.loop(0, tiles)
             def _(t):
                 columns = pl.ds(pl.multiple_of(t * tile, 128), tile)
                 total = jnp.dot(hid_a[c], down_w[j, :, columns], preferred_element_type=f32)
                 total += jnp.dot(hid_b[c], down_w[groups + j, :, columns], preferred_element_type=f32)
-                acc[:, columns] += total
-
-                @pl.when((j == groups - 1) & (b == 0))
-                def _():
-                    mine[:, columns] = acc[:, columns]
+
+                @pl.when(b == 0)
+                def _():
+                    mine[:, columns] += total
+
+                @pl.when(b > 0)
+                def _():
+                    acc[:, columns] += total
+
+                @pl.when(c == chunks - 1)
+                def _():
+                    out_copy(peers - 1, t, f).wait_recv()
+                    result[:, columns] = (mine[:, columns] + tok[peers - 1, :, columns].astype(f32)).astype(bf16)
+                    result_copy(t).start()
 
                 @pl.when((j == groups - 1) & (b > 0))
                 def _():
@@ -273,7 +310,7 @@
                     outgoing[lax.rem(b, 2), :, columns] = acc[:, columns].astype(bf16)
                     out_copy(b, t, peer).start()
 
-            @pl.when((j == min(2, groups - 1)) & (b > 1))
+            @pl.when((j == max(0, groups - 2)) & (b > 1))
             def _():
                 @pl.loop(0, tiles)
                 def _(t):
@@ -296,22 +333,20 @@
         first_matmuls(s + 1)
         second_matmul(s)
 
-    for t in range(tiles):
-        columns = pl.ds(t * tile, tile)
-        out_copy(peers - 1, t, f).wait_recv()
-        out[:, columns] = (mine[:, columns] + tok[peers - 1, :, columns].astype(f32)).astype(bf16)
     for p in range(1, peers):
         token_copy(p, f).wait_send()
     for p in range(max(1, peers - 2), peers):
         for t in range(tiles):
             out_copy(p, t, f).wait_send()
+    for t in range(tiles):
+        result_copy(t).wait()
 
 
 def on_device(n, peers, tokens, gate_weight, up_weight, down_weight):
     held, depth = tokens.shape
     hidden, width = down_weight.shape
     half = hidden // 2
-    cols = widest(half, 256)
+    cols = widest(half, COLS)
     groups = half // cols
     chunks = groups * peers
     bf16, f32 = jnp.bfloat16, jnp.float32
@@ -321,7 +356,7 @@
         functools.partial(kernel, n, peers),
         out_shape=jax.ShapeDtypeStruct((held, width), bf16),
         in_specs=[pl.BlockSpec(memory_space=pl.ANY)] * 4,
-        out_specs=pl.BlockSpec(memory_space=pltpu.VMEM),
+        out_specs=pl.BlockSpec(memory_space=pl.ANY),
         scratch_shapes=[
             pltpu.VMEM((peers, held, depth), bf16),
             pltpu.VMEM((2 * groups, depth, 2 * cols), bf16),
@@ -335,7 +370,8 @@
             pltpu.VMEM((held, width), f32),
             pltpu.VMEM((held, width), f32),
             pltpu.VMEM((2, held, width), bf16),
-            dma((2, 2, groups)), dma((2,)), dma((peers,)), dma((peers,)), dma((2, SENDS)), dma((2, SLOTS)),
+            pltpu.VMEM((held, width), bf16),
+            dma((2, 2, groups)), dma((2,)), dma((tiles,)), dma((peers,)), dma((peers,)), dma((2, SENDS)), dma((2, SLOTS)),
             regular((2,)), dma((2, SENDS)), dma((2, chunks)), dma((2, tiles)), dma((peers, tiles)), regular((peers,)),
         ],
         compiler_params=pltpu.CompilerParams(

time: 270 us -> 264 us (0.978)
  Pallas kernels: 268 us -> 262 us
    pallas_call x1, Pallas kernels: 268 us -> 262 us  [on_device(): pl.pallas_call(functools.partial(kernel, n, peers), out_shape=jax.ShapeDt...]
where the time goes in v2:
time: 264 us
  Pallas kernels  262 us (99%)
    pallas_call x1, Pallas kernels, on_device(): pl.pallas_call(functools.partial(kernel, n, peers), out_shape=jax.ShapeDt...  262 us

profile of v2, /device:TPU:0, one launch (start us, length us, event | category | flops | bytes accessed | tf_op | source)
XLA Modules:
  0.0 263.5 jit_solution(10656283844703376843)
XLA Ops:
  0.0 261.6 %shard_map.46 = bf16[128,2048]{1,0:T(8,128)(2,1)} custom-call(bf16[128,2048]{1,0:T(8,128)(2,1)} %tokens.1, bf16[2048,3584]{1,0:T(8,128)(2,1)} %w_gate.1, bf16[2048,3584]{1,0:T(8,128)(2,1)} %w_up.1, bf16[14,256,2048]{2,1,0:T(8,128)(2,1)} %bitcast.1), custom_call_target="tpu_custom_call" | custom-call | flops 45097156608 | bytes 44040192 | tf_op jit(solution)/shard_map/pallas_call | solution.py:355
  261.7 1.9 copy.6

commit v3 on v2

--- a/solution.py
+++ b/solution.py
@@ -8,9 +8,11 @@
 from jax.sharding import PartitionSpec as P
 
 SLOTS = 12
-STRIDE = 2
-LAG = 0
-SENDS = 3
+SUM_STRIDE = 1
+SUM_EXTRA = 1
+HID_STRIDE = 2
+PIECES = 2
+SENDS = 4
 PREFETCH = 2
 TAIL = 2
 COLS = 256
@@ -30,7 +32,7 @@
 
 
 def kernel(n, peers, tokens, w_gate, w_up, w_down, out, tok, first_w, down_w,
-           sum_a, sum_b, part_a, part_b, hid_a, hid_b, acc, mine, outgoing, result,
+           sum_a, sum_b, part_a, part_b, hid_a, hid_b, totals, outgoing, result,
            load_sem, own_sem, result_sem, tok_send, tok_recv, sum_send, sum_recv, credit, hid_send, hid_recv,
            out_send, out_recv, free):
     f32, bf16 = jnp.float32, jnp.bfloat16
@@ -38,7 +40,7 @@
     chunks, _, cols = hid_a.shape
     groups = chunks // peers
     half = groups * cols
-    width = acc.shape[1]
+    width = totals.shape[2]
     tile = widest(width, 512)
     tiles = width // tile
     last = n - 1
@@ -46,8 +48,16 @@
     others = (peers - 1) * groups
     sums, parts, hids = (sum_a, sum_b), (part_a, part_b), (hid_a, hid_b)
     depths = (m, last - m)
+    nearest, furthest = jnp.minimum(m, last - m), jnp.maximum(m, last - m)
+    rows = sum_a.shape[1] // PIECES
     ahead = (m + 1, m - 1)
     behind = (m - 1, m + 1)
+
+    def sum_step(depth):
+        return SUM_STRIDE * depth + SUM_EXTRA * jnp.minimum(depth, 1)
+
+    def hid_step(depth):
+        return HID_STRIDE * (2 * last - depth)
 
     def peer_of(p):
         return xor(f, jnp.where(p == peers - 1, 1, p + 1), peers)
@@ -99,11 +109,11 @@
             send_sem=tok_send.at[p], recv_sem=tok_recv.at[p],
             device_id={"ffn": peer}, device_id_type=MESH)
 
-    def sum_copy(d, c):
-        slot = lax.rem(c, SLOTS)
+    def sum_copy(d, c, k):
+        slot, piece = lax.rem(c, SLOTS), pl.ds(k * rows, rows)
         return pltpu.make_async_remote_copy(
-            src_ref=sums[d].at[slot], dst_ref=sums[d].at[slot],
-            send_sem=sum_send.at[d, lax.rem(c, SENDS)], recv_sem=sum_recv.at[d, slot],
+            src_ref=sums[d].at[slot, piece], dst_ref=sums[d].at[slot, piece],
+            send_sem=sum_send.at[d, lax.rem(c, SENDS), k], recv_sem=sum_recv.at[d, slot, k],
             device_id={"mp": ahead[d]}, device_id_type=MESH)
 
     def hid_copy(d, c):
@@ -113,14 +123,14 @@
             device_id={"mp": behind[d]}, device_id_type=MESH)
 
     def out_copy(p, t, peer):
-        columns = pl.ds(pl.multiple_of(t * tile, 128), tile)
+        columns = pl.ds(t * tile, tile)
         return pltpu.make_async_remote_copy(
             src_ref=outgoing.at[lax.rem(p, 2), :, columns], dst_ref=tok.at[p, :, columns],
             send_sem=out_send.at[lax.rem(p, 2), t], recv_sem=out_recv.at[p, t],
             device_id={"ffn": peer}, device_id_type=MESH)
 
     def result_copy(t):
-        columns = pl.ds(pl.multiple_of(t * tile, 128), tile)
+        columns = pl.ds(t * tile, tile)
         return pltpu.make_async_copy(result.at[:, columns], out.at[:, columns], result_sem.at[t])
 
     token_copy(1, peer_of(1)).start()
@@ -172,24 +182,25 @@
                 tok[b], first_w[d * groups + j], preferred_element_type=f32).astype(bf16)
 
     def first_matmuls(s):
-        b, j = place(s - STRIDE * jnp.minimum(depths[0], depths[1]))
+        b, j = place(s - sum_step(nearest))
 
         @pl.when((b > 0) & (j == 0))
         def _():
             token_copy(b, f).wait_recv()
 
         for d in range(2):
-            first_matmul(d, s - STRIDE * depths[d])
-
-        p, k = place(s - STRIDE * jnp.maximum(depths[0], depths[1]))
+            first_matmul(d, s - sum_step(depths[d]))
+
+        p, k = place(s - sum_step(furthest))
 
         @pl.when((p > 0) & (k == groups - 1))
         def _():
             pl.semaphore_signal(free.at[p], inc=1, device_id={"ffn": peer_of(p)}, device_id_type=MESH)
 
-    def pass_sum(d, s):
+    def pass_sum(d, k, s):
         depth, slots, part = depths[d], sums[d], parts[d]
-        c = s - STRIDE * depth
+        c = s - sum_step(depth)
+        piece = pl.ds(k * rows, rows)
 
         @pl.when((c >= 0) & (c < chunks))
         def _():
@@ -197,37 +208,40 @@
 
             @pl.when(depth > 0)
             def _():
-                sum_copy(d, c).wait_recv()
+                sum_copy(d, c, k).wait_recv()
 
             @pl.when(depth < last)
             def _():
-                @pl.when(c >= SLOTS)
-                def _():
-                    pl.semaphore_wait(credit.at[d], 1)
+                if k == 0:
+                    @pl.when(c >= SLOTS)
+                    def _():
+                        pl.semaphore_wait(credit.at[d], 1)
 
                 @pl.when(depth == 0)
                 def _():
-                    slots[slot] = part[...]
+                    slots[slot, piece, :] = part[piece, :]
 
                 @pl.when(depth > 0)
                 def _():
-                    slots[slot] = (slots[slot].astype(f32) + part[...].astype(f32)).astype(bf16)
-
-                sum_copy(d, c).start()
+                    total = slots[slot, piece, :].astype(f32) + part[piece, :].astype(f32)
+                    slots[slot, piece, :] = total.astype(bf16)
+
+                sum_copy(d, c, k).start()
 
             @pl.when(depth == last)
             def _():
-                gate = slots[slot, :, :cols].astype(f32) + part[:, :cols].astype(f32)
-                up = slots[slot, :, cols:].astype(f32) + part[:, cols:].astype(f32)
-                hids[d][c] = (gate / (1.0 + jnp.exp(-gate)) * up).astype(bf16)
-
-                @pl.when(c + SLOTS < chunks)
-                def _():
-                    pl.semaphore_signal(credit.at[d], inc=1, device_id={"mp": behind[d]}, device_id_type=MESH)
+                gate = slots[slot, piece, :cols].astype(f32) + part[piece, :cols].astype(f32)
+                up = slots[slot, piece, cols:].astype(f32) + part[piece, cols:].astype(f32)
+                hids[d][c, piece, :] = (gate / (1.0 + jnp.exp(-gate)) * up).astype(bf16)
+
+                if k == PIECES - 1:
+                    @pl.when(c + SLOTS < chunks)
+                    def _():
+                        pl.semaphore_signal(credit.at[d], inc=1, device_id={"mp": behind[d]}, device_id_type=MESH)
 
     def pass_hidden(d, s):
         depth = depths[d]
-        c = s - STRIDE * (2 * last - depth) - LAG
+        c = s - hid_step(depth)
 
         @pl.when((c >= 0) & (c < chunks))
         def _():
@@ -241,24 +255,25 @@
 
     def sent(d, s):
         depth = depths[d]
-        c = s - STRIDE * depth - (SENDS - 1)
+        c = s - sum_step(depth) - (SENDS - 1)
 
         @pl.when((depth < last) & (c >= 0) & (c < chunks))
         def _():
-            sum_copy(d, c).wait_send()
+            for k in range(PIECES):
+                sum_copy(d, c, k).wait_send()
 
             @pl.when((depth > 0) & (c + SLOTS < chunks))
             def _():
                 pl.semaphore_signal(credit.at[d], inc=1, device_id={"mp": behind[d]}, device_id_type=MESH)
 
-        h = s - STRIDE * (2 * last - depth) - LAG - (SENDS - 1)
+        h = s - hid_step(depth) - (SENDS - 1)
 
         @pl.when((depth > 0) & (h >= 0) & (h < chunks))
         def _():
             hid_copy(d, h).wait_send()
 
     def second_matmul(s):
-        c = s - STRIDE * jnp.maximum(2 * last - m, last + m) - LAG
+        c = s - hid_step(nearest)
 
         @pl.when(c == 0)
         def _():
@@ -269,68 +284,58 @@
             b, j = place(c)
             peer = peer_of(b)
 
+            to = jnp.minimum(b, 1)
+
+            @pl.when(j == 0)
+            def _():
+                totals[to] = jnp.zeros(totals.shape[1:], f32)
+
+            product = jnp.dot(hid_a[c], down_w[j], preferred_element_type=f32)
+            product += jnp.dot(hid_b[c], down_w[groups + j], preferred_element_type=f32)
+            totals[to] += product
+
+            @pl.when(c == chunks - 1)
+            def _():
+                for t in range(tiles):
+                    columns = pl.ds(t * tile, tile)
+                    out_copy(peers - 1, t, f).wait_recv()
+                    total = totals[0, :, columns] + tok[peers - 1, :, columns].astype(f32)
+                    result[:, columns] = total.astype(bf16)
+                    result_copy(t).start()
+
             @pl.when((j == groups - 1) & (b > 0))
             def _():
                 pl.semaphore_wait(free.at[b], 1)
-
-            @pl.when((j == 0) & (b > 0))
-            def _():
-                acc[...] = jnp.zeros_like(acc)
-
-            @pl.when(c == 0)
-            def _():
-                mine[...] = jnp.zeros_like(mine)
-
-            @pl.loop(0, tiles)
-            def _(t):
-                columns = pl.ds(pl.multiple_of(t * tile, 128), tile)
-                total = jnp.dot(hid_a[c], down_w[j, :, columns], preferred_element_type=f32)
-                total += jnp.dot(hid_b[c], down_w[groups + j, :, columns], preferred_element_type=f32)
-
-                @pl.when(b == 0)
-                def _():
-                    mine[:, columns] += total
-
-                @pl.when(b > 0)
-                def _():
-                    acc[:, columns] += total
-
-                @pl.when(c == chunks - 1)
-                def _():
-                    out_copy(peers - 1, t, f).wait_recv()
-                    result[:, columns] = (mine[:, columns] + tok[peers - 1, :, columns].astype(f32)).astype(bf16)
-                    result_copy(t).start()
-
-                @pl.when((j == groups - 1) & (b > 0))
-                def _():
+                for t in range(tiles):
                     @pl.when(b > 2)
                     def _():
                         out_copy(b - 2, t, peer).wait_send()
 
-                    outgoing[lax.rem(b, 2), :, columns] = acc[:, columns].astype(bf16)
+                    columns = pl.ds(t * tile, tile)
+                    outgoing[lax.rem(b, 2), :, columns] = totals[1, :, columns].astype(bf16)
                     out_copy(b, t, peer).start()
 
             @pl.when((j == max(0, groups - 2)) & (b > 1))
             def _():
-                @pl.loop(0, tiles)
-                def _(t):
-                    columns = pl.ds(pl.multiple_of(t * tile, 128), tile)
+                for t in range(tiles):
+                    columns = pl.ds(t * tile, tile)
                     out_copy(b - 1, t, f).wait_recv()
-                    mine[:, columns] += tok[b - 1, :, columns].astype(f32)
+                    totals[0, :, columns] += tok[b - 1, :, columns].astype(f32)
 
     own_load.wait()
     first_matmuls(jnp.int32(0))
 
-    @pl.loop(0, chunks + 2 * STRIDE * last + LAG + max(0, SENDS - 1 - STRIDE))
+    @pl.loop(0, chunks + 2 * HID_STRIDE * last + max(0, SENDS - 1 - HID_STRIDE))
     def _(s):
+        for k in range(PIECES):
+            pass_sum(0, k, s)
+            pass_sum(1, k, s)
+        pass_hidden(0, s)
+        pass_hidden(1, s)
         start_loads(s)
-        pass_sum(0, s)
-        pass_sum(1, s)
+        first_matmuls(s + 1)
         sent(0, s)
         sent(1, s)
-        pass_hidden(0, s)
-        pass_hidden(1, s)
-        first_matmuls(s + 1)
         second_matmul(s)
 
     for p in range(1, peers):
@@ -367,11 +372,10 @@
             pltpu.VMEM((held, 2 * cols), bf16),
             pltpu.VMEM((chunks, held, cols), bf16),
             pltpu.VMEM((chunks, held, cols), bf16),
-            pltpu.VMEM((held, width), f32),
-            pltpu.VMEM((held, width), f32),
+            pltpu.VMEM((2, held, width), f32),
             pltpu.VMEM((2, held, width), bf16),
             pltpu.VMEM((held, width), bf16),
-            dma((2, 2, groups)), dma((2,)), dma((tiles,)), dma((peers,)), dma((peers,)), dma((2, SENDS)), dma((2, SLOTS)),
+            dma((2, 2, groups)), dma((2,)), dma((tiles,)), dma((peers,)), dma((peers,)), dma((2, SENDS, PIECES)), dma((2, SLOTS, PIECES)),
             regular((2,)), dma((2, SENDS)), dma((2, chunks)), dma((2, tiles)), dma((peers, tiles)), regular((peers,)),
         ],
         compiler_params=pltpu.CompilerParams(

time: 264 us -> 262 us (level)
  no operation moved by 1% of the time
where the time goes in v3:
time: 262 us
  Pallas kernels  260 us (99%)
    pallas_call x1, Pallas kernels, on_device(): pl.pallas_call(functools.partial(kernel, n, peers), out_shape=jax.ShapeDt...  260 us

profile of v3, /device:TPU:0, one launch (start us, length us, event | category | flops | bytes accessed | tf_op | source)
XLA Modules:
  0.0 262.0 jit_solution(2137848901955630573)
XLA Ops:
  0.0 260.1 %shard_map.46 = bf16[128,2048]{1,0:T(8,128)(2,1)} custom-call(bf16[128,2048]{1,0:T(8,128)(2,1)} %tokens.1, bf16[2048,3584]{1,0:T(8,128)(2,1)} %w_gate.1, bf16[2048,3584]{1,0:T(8,128)(2,1)} %w_up.1, bf16[14,256,2048]{2,1,0:T(8,128)(2,1)} %bitcast.1), custom_call_target="tpu_custom_call" | custom-call | flops 45097156608 | bytes 44040192 | tf_op jit(solution)/shard_map/pallas_call | solution.py:360
  260.1 1.9 copy.6

commit v4 on v3

--- a/solution.py
+++ b/solution.py
@@ -11,7 +11,7 @@
 SUM_STRIDE = 1
 SUM_EXTRA = 1
 HID_STRIDE = 2
-PIECES = 2
+PIECES = 4
 SENDS = 4
 PREFETCH = 2
 TAIL = 2

time: 262 us -> 261 us (level)
  no operation moved by 1% of the time
where the time goes in v4:
time: 261 us
  Pallas kernels  259 us (99%)
    pallas_call x1, Pallas kernels, on_device(): pl.pallas_call(functools.partial(kernel, n, peers), out_shape=jax.ShapeDt...  259 us

profile of v4, /device:TPU:0, one launch (start us, length us, event | category | flops | bytes accessed | tf_op | source)
XLA Modules:
  0.0 261.1 jit_solution(13162344412246000493)
XLA Ops:
  0.0 259.2 %shard_map.46 = bf16[128,2048]{1,0:T(8,128)(2,1)} custom-call(bf16[128,2048]{1,0:T(8,128)(2,1)} %tokens.1, bf16[2048,3584]{1,0:T(8,128)(2,1)} %w_gate.1, bf16[2048,3584]{1,0:T(8,128)(2,1)} %w_up.1, bf16[14,256,2048]{2,1,0:T(8,128)(2,1)} %bitcast.1), custom_call_target="tpu_custom_call" | custom-call | flops 45097156608 | bytes 44040192 | tf_op jit(solution)/shard_map/pallas_call | solution.py:360
  259.2 1.9 copy.6
